TPU v7x, 256 devices: a whole 4x4x8 slice. The times are simulated.
256 devices in a mesh: grp: 8 (over z_lo, core), dev: 32 (over y, x, z_hi).
Axes of the slice: x: 4, y: 4, z: 8 (z_hi: 2, z_lo: 4; z = z_hi * 4 + z_lo), core: 2. Of those that a mesh axis runs over, the one named last changes fastest.
Arguments:
- spectra: bfloat16 [4096, 16, 256], P(('grp', 'dev')), may hold values from -6 to 6
- round_mask: int32 [1], replicated, may hold values from 0 to 32767
Outputs:
- correlations: bfloat16 [768, 4096, 512], P(None, ('grp', 'dev'))
All inputs are finite; a program needn't handle non-finite values.
Results may differ from a plain program's by a relative error of at most 0.0056.
Values may be sent and summed in bfloat16 or wider, within the bound.
A program may use at most 128 MiB of HBM per device.

v0:
```python
import functools
import math

import jax
import jax.numpy as jnp
import numpy as np
from jax import lax
from jax.experimental import pallas as pl
from jax.experimental.pallas import tpu as pltpu
from jax.sharding import PartitionSpec as P

MESH = pl.DeviceIdType.MESH
NF = 256
WINDOWS = 8
LAGS = 768
HALF = LAGS // 2
FREQ_LO = 64
NFFT = 1024
ROWS = 400
CH = 16
PIECES = 4
F32, BF16 = jnp.float32, jnp.bfloat16


def make_tables():
    freq = np.arange(NF)
    steps = ((FREQ_LO + freq)[None, :] * np.arange(ROWS)[:, None]) % NFFT
    theta = 2.0 * math.pi / NFFT * steps
    taper = (0.5 - 0.5 * np.cos(2.0 * math.pi * (freq + 0.5) / NF)) / math.sqrt(2.0 * WINDOWS * NF)
    return np.stack([taper * np.cos(theta), -taper * np.sin(theta)]).astype(jnp.bfloat16)


def prepare(x_ref, xs, send):
    for half in range(2):
        xs[half] = x_ref[:, :, half * 128 : half * 128 + 128].reshape(256, 128).astype(F32)
    lane = lax.broadcasted_iota(jnp.int32, (CH, 128), 1) // 16
    for half in range(2):
        for h in range(2):
            rows = [xs[half, pl.ds(8 * h + w, CH, stride=16), :] for w in range(8)]
            for g in range(8):
                acc = None
                for w in range(8):
                    shift = ((w - g) * 16) % 128
                    v = rows[w] if shift == 0 else pltpu.roll(rows[w], shift, 1)
                    acc = v if acc is None else jnp.where(lane == w, v, acc)
                first = g * 256 + h * 128
                send[half, :, first : first + 128] = acc.astype(BF16)


def build_diag(send, diag):
    mask = (lax.broadcasted_iota(jnp.int32, (16, 128), 1) % 16) == lax.broadcasted_iota(jnp.int32, (16, 128), 0)
    for half in range(2):

        def body(g, carry):
            base = pl.multiple_of(g * 256, 256)
            lo = send[half, :, pl.ds(base, 128)].astype(F32)
            hi = send[half, :, pl.ds(base + 128, 128)].astype(F32)
            for c in range(CH):
                re = jnp.where(mask, jnp.broadcast_to(lo[c : c + 1], (16, 128)), 0.0)
                im = jnp.where(mask, jnp.broadcast_to(hi[c : c + 1], (16, 128)), 0.0)
                r0 = c * 32
                diag[half * 8 + g, r0 : r0 + 16, 0:128] = re.astype(BF16)
                diag[half * 8 + g, r0 : r0 + 16, 128:256] = im.astype(BF16)
                diag[half * 8 + g, r0 + 16 : r0 + 32, 0:128] = im.astype(BF16)
                diag[half * 8 + g, r0 + 16 : r0 + 32, 128:256] = (-re).astype(BF16)
            return carry

        lax.fori_loop(0, 8, body, 0)


def cross_half(whole, diag, cross, row, half):
    def body(g, carry):
        right = whole[half, pl.ds(row, 128), pl.ds(pl.multiple_of(g * 256, 256), 256)]
        gg = half * 8 + g
        k0 = pl.multiple_of(gg * 16, 16)
        res = lax.dot_general(diag[gg], right, (((1,), (1,)), ((), ())), preferred_element_type=F32).astype(BF16)
        for c in range(CH):
            for r in range(2):
                r0 = c * 32 + r * 16
                cross[r, c // 2, pl.ds(k0, 16), (c % 2) * 128 : (c % 2) * 128 + 128] = res[r0 : r0 + 16]
        return carry

    lax.fori_loop(0, 8, body, 0, unroll=4)


def lags_of(table, cross, scr):
    def body(cp, carry):
        even = jnp.dot(table[0], cross[0, cp], preferred_element_type=F32)
        odd = jnp.dot(table[1], cross[1, cp], preferred_element_type=F32)
        later, earlier = even + odd, even - odd
        for b in range(2):
            scr[0, pl.ds(2 * cp + b, ROWS, stride=CH), :] = later[:, b * 128 : b * 128 + 128]
            scr[1, pl.ds(2 * cp + b, ROWS, stride=CH), :] = earlier[:, b * 128 : b * 128 + 128]
        return carry

    lax.fori_loop(0, 8, body, 0, unroll=2)


def finish(scr, out):
    def body(i, carry):
        for u in range(8):
            d = i * 8 + u
            out[HALF + d] = scr[0, pl.ds(pl.multiple_of(d * CH, CH), CH), :].astype(BF16)
            out[HALF - 1 - d] = scr[1, pl.ds(pl.multiple_of(d * CH + CH, CH), CH), :].astype(BF16)
        return carry

    lax.fori_loop(0, HALF // 8, body, 0)


def flip(z_lo, bits):
    if bits & 1:
        z_lo = z_lo + 1 - 2 * lax.rem(z_lo, 2)
    if bits & 2:
        z_lo = lax.rem(z_lo + 2, 4)
    return z_lo


OFFSETS = (0, -1, 1, 2)


def parts_of(half, dx, dy):
    first, second = (dx, dy) if half == 0 else (dy, dx)
    if second == 2 or (second == 0 and first == 2):
        return ("a", "b")
    return ("ab",)


KEYS = {}
for _half in range(2):
    for _dx in OFFSETS:
        for _dy in OFFSETS:
            if (_dx, _dy) != (0, 0):
                for _part in parts_of(_half, _dx, _dy):
                    KEYS[_half, _dx, _dy, _part] = len(KEYS)

def wrap(offset):
    offset %= 4
    return offset - 4 if offset == 3 else offset


def swap_kernel(code, x_ref, own, pair, xs, land, send_sem, recv_sem):
    grp, dev = lax.axis_index("grp"), lax.axis_index("dev")
    z_lo, core, z_hi = grp // 2, lax.rem(grp, 2), lax.rem(dev, 2)
    partner = flip(z_lo, code >> 1) * 2 + (1 - core if code & 1 else core)
    sides = [(partner, dev), (partner, dev + 1 - 2 * z_hi)]
    active = [1] if code == 0 else [0, 1]

    barrier = pltpu.get_barrier_semaphore()
    for side in active:
        pl.semaphore_signal(barrier, inc=1, device_id=sides[side], device_id_type=MESH)
    prepare(x_ref, xs, own)
    pl.semaphore_wait(barrier, len(active))

    copies = []
    for half in range(2):
        for side in active:
            k = half * 2 + side
            copies.append(pltpu.make_async_remote_copy(
                src_ref=own.at[half], dst_ref=land.at[side, half], send_sem=send_sem.at[k], recv_sem=recv_sem.at[k],
                device_id=sides[side], device_id_type=MESH,
            ))
            copies[-1].start()
    same = pl.multiple_of(z_hi * 16, 16)
    far = pl.multiple_of(16 - z_hi * 16, 16)
    if code == 0:
        for half in range(2):
            pair[half, pl.ds(same, 16), :] = own[half]
    for c in copies:
        c.wait()
    for half in range(2):
        for side in active:
            pair[half, pl.ds(same if side == 0 else far, 16), :] = land[side, half]


def gather_kernel(own, pair, table_hbm, tiles, last, table, diag, whole, cross, scr, send_sem, recv_sem, table_sem):
    grp, dev = lax.axis_index("grp"), lax.axis_index("dev")
    y, x, z_hi = dev // 8, lax.rem(dev // 2, 4), lax.rem(dev, 2)

    def at(off_x, off_y):
        return grp, lax.rem(y + off_y + 4, 4) * 8 + lax.rem(x + off_x + 4, 4) * 2 + z_hi

    steps = {("x", 1): at(1, 0), ("x", -1): at(-1, 0), ("y", 1): at(0, 1), ("y", -1): at(0, -1)}
    fetch = pltpu.make_async_copy(table_hbm, table, table_sem)
    fetch.start()
    barrier = pltpu.get_barrier_semaphore()
    for device in steps.values():
        pl.semaphore_signal(barrier, inc=1, device_id=device, device_id_type=MESH)
    for half in range(2):
        whole[half, pl.ds(pl.multiple_of((y * 8 + x * 2) * 16, 32), 32), :] = pair[half]
    pl.semaphore_wait(barrier, 4)

    started = []

    def block(half, dx, dy, part):
        row = (lax.rem(y + dy + 4, 4) * 8 + lax.rem(x + dx + 4, 4) * 2) * 16
        if part == "ab":
            return whole.at[half, pl.ds(pl.multiple_of(row, 32), 32), :]
        return whole.at[half, pl.ds(pl.multiple_of(row + (16 if part == "b" else 0), 16), 16), :]

    def copy(half, dx, dy, part, k, device):
        ref = block(half, dx, dy, part)
        return pltpu.make_async_remote_copy(
            src_ref=ref, dst_ref=ref, send_sem=send_sem.at[k], recv_sem=recv_sem.at[k],
            device_id=device, device_id_type=MESH,
        )

    def push(half, dx, dy, part, axis, way):
        to = (wrap(dx - way), dy) if axis == "x" else (dx, wrap(dy - way))
        c = copy(half, dx, dy, part, KEYS[half, to[0], to[1], part], steps[axis, way])
        c.start()
        started.append(c)

    def arrive(half, dx, dy):
        for part in parts_of(half, dx, dy):
            copy(half, dx, dy, part, KEYS[half, dx, dy, part], steps["x", 1]).wait_recv()

    axes = (("x", "y"), ("y", "x"))

    def swap(half, a, b):
        return (a, b) if half == 0 else (b, a)

    def send_full(half, a, b, which):
        dx, dy = swap(half, a, b)
        for way in (1, -1):
            push(half, dx, dy, "ab", axes[half][which], way)

    def forward(half, a, b, which):
        dx, dy = swap(half, a, b)
        came = (a, b)[which]
        push(half, dx, dy, "a" if came == -1 else "b", axes[half][which], -came)

    def take(half, a, b):
        arrive(half, *swap(half, a, b))

    for half in range(2):
        send_full(half, 0, 0, 0)
        send_full(half, 0, 0, 1)
    build_diag(own, diag)
    for half in range(2):
        for a in (-1, 1):
            take(half, a, 0)
            forward(half, a, 0, 0)
            send_full(half, a, 0, 1)
    for half in range(2):
        for b in (-1, 1):
            take(half, 0, b)
            forward(half, 0, b, 1)
    for half in range(2):
        take(half, 2, 0)
        send_full(half, 2, 0, 1)

    def row_of(dy):
        return pl.multiple_of(lax.rem(y + dy + 4, 4) * 128, 128)

    fetch.wait()
    cross_half(whole, diag, cross, row_of(0), 0)
    for half in range(2):
        for a in (-1, 1):
            for b in (-1, 1):
                take(half, a, b)
                forward(half, a, b, 1)
    arrive(1, 2, 0)
    cross_half(whole, diag, cross, row_of(0), 1)
    lags_of(table, cross, scr)
    for half in range(2):
        for b in (-1, 1):
            take(half, 2, b)
            forward(half, 2, b, 1)
    finish(scr, tiles.at[0])
    for i, dy in enumerate((-1, 1)):
        cross_half(whole, diag, cross, row_of(dy), 0)
        arrive(1, 2, dy)
        cross_half(whole, diag, cross, row_of(dy), 1)
        lags_of(table, cross, scr)
        finish(scr, tiles.at[1 + i])
    for dx in OFFSETS:
        arrive(0, dx, 2)
    cross_half(whole, diag, last, row_of(2), 0)
    arrive(1, 2, 2)
    cross_half(whole, diag, last, row_of(2), 1)
    for c in started:
        c.wait_send()


def write_kernel(tiles, last, table, out, scr, stage, sem):
    y = lax.axis_index("dev") // 8

    def put(src, dy, k):
        lanes = pl.multiple_of(lax.rem(y + dy + 4, 4) * 128, 128)
        part = LAGS // PIECES
        return [
            pltpu.make_async_copy(
                src.at[pl.ds(i * part, part)], out.at[pl.ds(i * part, part), :, pl.ds(lanes, 128)], sem.at[k * PIECES + i]
            )
            for i in range(PIECES)
        ]

    copies = []
    for i, dy in enumerate((0, -1, 1)):
        copies += put(tiles.at[i], dy, i)
    for c in copies:
        c.start()
    lags_of(table, last, scr)
    finish(scr, stage)
    final = put(stage, 2, 3)
    for c in final:
        c.start()
    for c in copies + final:
        c.wait()


def on_device(spectra, round_mask):
    mask = jnp.mod(round_mask[0], lax.axis_size("grp"))
    table = jnp.asarray(make_tables())
    vmem = pl.BlockSpec(memory_space=pltpu.VMEM)

    def swap(code, block):
        return pl.pallas_call(
            functools.partial(swap_kernel, code),
            out_shape=(pltpu.VMEM((2, CH, 2048), BF16), pltpu.VMEM((2, 2 * CH, 2048), BF16)),
            in_specs=[vmem],
            out_specs=(vmem, vmem),
            scratch_shapes=[
                pltpu.VMEM((2, 256, 128), F32),
                pltpu.VMEM((2, 2, CH, 2048), BF16),
                pltpu.SemaphoreType.DMA((4,)),
                pltpu.SemaphoreType.DMA((4,)),
            ],
            compiler_params=pltpu.CompilerParams(
                collective_id=code, has_side_effects=True, vmem_limit_bytes=8 * 2**20
            ),
            name=f"swap_{code}",
        )(block)

    own, pair = lax.switch(mask, [functools.partial(swap, code) for code in range(8)], spectra)
    tiles, last, table = pl.pallas_call(
        gather_kernel,
        out_shape=(
            pltpu.VMEM((3, LAGS, CH, 128), BF16),
            pltpu.VMEM((2, 8, NF, 256), BF16),
            pltpu.VMEM((2, ROWS, NF), BF16),
        ),
        in_specs=[vmem, vmem, pl.BlockSpec(memory_space=pltpu.HBM)],
        out_specs=(vmem, vmem, vmem),
        scratch_shapes=[
            pltpu.VMEM((16, 512, 256), BF16),
            pltpu.VMEM((2, 512, 2048), BF16),
            pltpu.VMEM((2, 8, NF, 256), BF16),
            pltpu.VMEM((2, ROWS * CH, 128), F32),
            pltpu.SemaphoreType.DMA((len(KEYS),)),
            pltpu.SemaphoreType.DMA((len(KEYS),)),
            pltpu.SemaphoreType.DMA,
        ],
        compiler_params=pltpu.CompilerParams(collective_id=8, has_side_effects=True, vmem_limit_bytes=24 * 2**20),
        name="gather",
    )(own, pair, table)
    return pl.pallas_call(
        write_kernel,
        out_shape=jax.ShapeDtypeStruct((LAGS, CH, 512), BF16),
        in_specs=[vmem] * 3,
        out_specs=pl.BlockSpec(memory_space=pl.ANY),
        scratch_shapes=[
            pltpu.VMEM((2, ROWS * CH, 128), F32),
            pltpu.VMEM((LAGS, CH, 128), BF16),
            pltpu.SemaphoreType.DMA((4 * PIECES,)),
        ],
        compiler_params=pltpu.CompilerParams(vmem_limit_bytes=24 * 2**20),
        name="write",
    )(tiles, last, table)


def solution(mesh):
    return jax.shard_map(
        on_device,
        mesh=mesh,
        in_specs=(P(("grp", "dev"), None, None), P()),
        out_specs=P(None, ("grp", "dev"), None),
        check_vma=False,
    )
```

profile of v0, /device:TPU:32, one launch (start us, length us, event | category | flops | bytes accessed | tf_op | source)
XLA Modules:
  0.0 62.0 jit_solution(5767329248383924693)
XLA Ops:
  0.7 14.6 %conditional.1 = ((bf16[2,16,2048]{2,1,0:T(8,128)(2,1)S(1)}, bf16[2,32,2048]{2,1,0:T(8,128)(2,1)S(1)})) conditional(s32[]{:T(128)} %clamp.3, bf16[16,16,256]{2,1,0:T(8,128)(2,1)} %param.11, bf16[16,16,256]{2,1,0:T(8,128)(2,1)} %param.11, bf16[16,16,256]{2,1,0:T(8,128)(2,1)} %param.11, ...), branch_computations={%region_0.1_spmd, %region_1.2_spmd, %region_2.3_spmd, %region_3.4_... | conditional | bytes 8 | solution.py:335
  0.7 14.5 %swap_5.1 = (bf16[2,16,2048]{2,1,0:T(8,128)(2,1)S(1)}, bf16[2,32,2048]{2,1,0:T(8,128)(2,1)S(1)}) custom-call(bf16[16,16,256]{2,1,0:T(8,128)(2,1)} %x_ref.5), custom_call_target="tpu_custom_call" | custom-call | tf_op jit(solution)/shard_map/cond/branch_5_fun/swap_5/pallas_call | solution.py:318
  15.3 0.0 copy-start
  15.3 1.0 %copy-done = bf16[2,400,256]{2,1,0:T(8,128)(2,1)S(1)} copy-done((bf16[2,400,256]{2,1,0:T(8,128)(2,1)S(1)}, bf16[2,400,256]{2,1,0:T(8,128)(2,1)}, u32[]{:S(2)}) %copy-start) | copy-done | bytes 409624
  16.3 40.0 %gather.1 = (bf16[3,768,16,128]{3,2,1,0:T(8,128)(2,1)S(1)}, bf16[2,8,256,256]{3,2,1,0:T(8,128)(2,1)S(1)}, bf16[2,400,256]{2,1,0:T(8,128)(2,1)S(1)}) custom-call(bf16[2,16,2048]{2,1,0:T(8,128)(2,1)S(1)} %get-tuple-element.18.own, bf16[2,32,2048]{2,1,0:T(8,128)(2,1)S(1)} %get-tuple-element.19.pair, bf16[2,400,256]{2,1,0:T(8,128)(2,1)S(1)} %copy-done), custom_call_target="tpu_custom_call" | custom-call | tf_op jit(solution)/shard_map/gather/pallas_call | solution.py:336
  56.3 5.7 %write.1 = bf16[768,16,512]{2,1,0:T(8,128)(2,1)} custom-call(bf16[3,768,16,128]{3,2,1,0:T(8,128)(2,1)S(1)} %get-tuple-element.20.tiles, bf16[2,8,256,256]{3,2,1,0:T(8,128)(2,1)S(1)} %get-tuple-element.21.last, bf16[2,400,256]{2,1,0:T(8,128)(2,1)S(1)} %get-tuple-element.22.table), custom_call_target="tpu_custom_call" | custom-call | tf_op jit(solution)/shard_map/write/pallas_call | solution.py:357
Async XLA Ops:
  15.3 1.0 %copy-start = (bf16[2,400,256]{2,1,0:T(8,128)(2,1)S(1)}, bf16[2,400,256]{2,1,0:T(8,128)(2,1)}, u32[]{:S(2)}) copy-start(bf16[2,400,256]{2,1,0:T(8,128)(2,1)} %constant.17.clone.table_hbm) | copy-start | bytes 1228804
where the time goes:
time: 62.5 us; the launch traced here: 62 us
  Pallas kernels  60.2 us (96%)
  local copies, waits for them, and re-layouts  1 us (2%)
  between operations  0.69 us (1%)
    pallas_call x1, Pallas kernels, on_device(): pl.pallas_call(gather_kernel, out_shape=(pltpu.VMEM((3, LAGS, CH, 128), B...  40 us
    pallas_call x1, Pallas kernels, swap(): pl.pallas_call(functools.partial(swap_kernel, code), out_shape=(pltpu.VME...  14.5 us
    pallas_call x1, Pallas kernels, on_device(): pl.pallas_call(write_kernel, out_shape=jax.ShapeDtypeStruct((LAGS, CH, 51...  5.66 us

commit v1 on v0

--- a/solution.py
+++ b/solution.py
@@ -80,31 +80,64 @@
                 cross[r, c // 2, pl.ds(k0, 16), (c % 2) * 128 : (c % 2) * 128 + 128] = res[r0 : r0 + 16]
         return carry
 
-    lax.fori_loop(0, 8, body, 0, unroll=4)
+    lax.fori_loop(0, 8, body, 0, unroll=8)
+
+
+def cross_pair(whole, diag, cross, row, row2, half):
+    def body(g, carry):
+        cols = pl.ds(pl.multiple_of(g * 256, 256), 256)
+        right = jnp.concatenate([whole[half, pl.ds(row, 128), cols], whole[half, pl.ds(row2, 128), cols]], axis=0)
+        gg = half * 8 + g
+        k0 = pl.multiple_of(gg * 16, 16)
+        res = lax.dot_general(diag[gg], right, (((1,), (1,)), ((), ())), preferred_element_type=F32).astype(BF16)
+        for c in range(CH):
+            for r in range(2):
+                r0 = c * 32 + r * 16
+                cross[r, c, pl.ds(k0, 16), :] = res[r0 : r0 + 16]
+        return carry
+
+    lax.fori_loop(0, 8, body, 0, unroll=8)
+
+
+def both_sides(table, re, im):
+    even = jnp.dot(table[0], re, preferred_element_type=F32)
+    odd = jnp.dot(table[1], im, preferred_element_type=F32)
+    return (even + odd).astype(BF16), (even - odd).astype(BF16)
 
 
 def lags_of(table, cross, scr):
     def body(cp, carry):
-        even = jnp.dot(table[0], cross[0, cp], preferred_element_type=F32)
-        odd = jnp.dot(table[1], cross[1, cp], preferred_element_type=F32)
-        later, earlier = even + odd, even - odd
+        later, earlier = both_sides(table, cross[0, cp], cross[1, cp])
         for b in range(2):
-            scr[0, pl.ds(2 * cp + b, ROWS, stride=CH), :] = later[:, b * 128 : b * 128 + 128]
-            scr[1, pl.ds(2 * cp + b, ROWS, stride=CH), :] = earlier[:, b * 128 : b * 128 + 128]
+            scr[0, 2 * cp + b] = later[:, b * 128 : b * 128 + 128]
+            scr[1, 2 * cp + b] = earlier[:, b * 128 : b * 128 + 128]
         return carry
 
-    lax.fori_loop(0, 8, body, 0, unroll=2)
+    lax.fori_loop(0, 8, body, 0, unroll=4)
+
+
+def lags_pair(table, cross, scr):
+    def body(c, carry):
+        later, earlier = both_sides(table, cross[0, c], cross[1, c])
+        for b in range(2):
+            scr[b, 0, c] = later[:, b * 128 : b * 128 + 128]
+            scr[b, 1, c] = earlier[:, b * 128 : b * 128 + 128]
+        return carry
+
+    lax.fori_loop(0, CH, body, 0, unroll=4)
 
 
 def finish(scr, out):
     def body(i, carry):
-        for u in range(8):
-            d = i * 8 + u
-            out[HALF + d] = scr[0, pl.ds(pl.multiple_of(d * CH, CH), CH), :].astype(BF16)
-            out[HALF - 1 - d] = scr[1, pl.ds(pl.multiple_of(d * CH + CH, CH), CH), :].astype(BF16)
+        d = pl.multiple_of(i * 16, 16)
+        out[pl.ds(HALF + d, 16)] = jnp.swapaxes(scr[0, :, pl.ds(d, 16), :], 0, 1)
+        earlier = jnp.swapaxes(scr[1, :, pl.ds(d, 16), :], 0, 1)
+        for u in range(16):
+            out[HALF - d - u] = earlier[u]
         return carry
 
-    lax.fori_loop(0, HALF // 8, body, 0)
+    lax.fori_loop(0, HALF // 16, body, 0, unroll=2)
+    out[0] = jnp.swapaxes(scr[1, :, HALF : HALF + 16, :], 0, 1)[0]
 
 
 def flip(z_lo, bits):
@@ -253,26 +286,28 @@
         return pl.multiple_of(lax.rem(y + dy + 4, 4) * 128, 128)
 
     fetch.wait()
-    cross_half(whole, diag, cross, row_of(0), 0)
+    first = cross.at[:, 0:8]
+    cross_half(whole, diag, first, row_of(0), 0)
     for half in range(2):
         for a in (-1, 1):
             for b in (-1, 1):
                 take(half, a, b)
                 forward(half, a, b, 1)
     arrive(1, 2, 0)
-    cross_half(whole, diag, cross, row_of(0), 1)
-    lags_of(table, cross, scr)
+    cross_half(whole, diag, first, row_of(0), 1)
     for half in range(2):
         for b in (-1, 1):
             take(half, 2, b)
             forward(half, 2, b, 1)
-    finish(scr, tiles.at[0])
-    for i, dy in enumerate((-1, 1)):
-        cross_half(whole, diag, cross, row_of(dy), 0)
-        arrive(1, 2, dy)
-        cross_half(whole, diag, cross, row_of(dy), 1)
-        lags_of(table, cross, scr)
-        finish(scr, tiles.at[1 + i])
+    lags_of(table, first, scr.at[0])
+    finish(scr.at[0], tiles.at[0])
+    cross_pair(whole, diag, cross, row_of(-1), row_of(1), 0)
+    arrive(1, 2, -1)
+    arrive(1, 2, 1)
+    cross_pair(whole, diag, cross, row_of(-1), row_of(1), 1)
+    lags_pair(table, cross, scr)
+    finish(scr.at[0], tiles.at[1])
+    finish(scr.at[1], tiles.at[2])
     for dx in OFFSETS:
         arrive(0, dx, 2)
     cross_half(whole, diag, last, row_of(2), 0)
@@ -345,22 +380,22 @@
         scratch_shapes=[
             pltpu.VMEM((16, 512, 256), BF16),
             pltpu.VMEM((2, 512, 2048), BF16),
-            pltpu.VMEM((2, 8, NF, 256), BF16),
-            pltpu.VMEM((2, ROWS * CH, 128), F32),
+            pltpu.VMEM((2, CH, NF, 256), BF16),
+            pltpu.VMEM((2, 2, CH, ROWS, 128), BF16),
             pltpu.SemaphoreType.DMA((len(KEYS),)),
             pltpu.SemaphoreType.DMA((len(KEYS),)),
             pltpu.SemaphoreType.DMA,
         ],
         compiler_params=pltpu.CompilerParams(collective_id=8, has_side_effects=True, vmem_limit_bytes=24 * 2**20),
         name="gather",
-    )(own, pair, table)
+    )(own, pair, pltpu.with_memory_space_constraint(table, pltpu.HBM))
     return pl.pallas_call(
         write_kernel,
         out_shape=jax.ShapeDtypeStruct((LAGS, CH, 512), BF16),
         in_specs=[vmem] * 3,
         out_specs=pl.BlockSpec(memory_space=pl.ANY),
         scratch_shapes=[
-            pltpu.VMEM((2, ROWS * CH, 128), F32),
+            pltpu.VMEM((2, CH, ROWS, 128), BF16),
             pltpu.VMEM((LAGS, CH, 128), BF16),
             pltpu.SemaphoreType.DMA((4 * PIECES,)),
         ],

time: 62.5 us -> 55.3 us (0.88)
  Pallas kernels: 60.2 us -> 54.4 us
  local copies, waits for them, and re-layouts: 1 us -> 0 us
    pallas_call x1, Pallas kernels: 40 us -> 35.7 us  [on_device(): pl.pallas_call(gather_kernel, out_shape=(pltpu.VMEM((3, LAGS, CH, 128), B...]
    unnamed x2 -> x0, local copies, waits for them, and re-layouts: 1 us -> none
    pallas_call x1, Pallas kernels: 5.66 us -> 4.72 us  [on_device(): pl.pallas_call(write_kernel, out_shape=jax.ShapeDtypeStruct((LAGS, CH, 51...]
where the time goes in v1:
time: 55.3 us; the launch traced here: 55.2 us
  Pallas kernels  54.4 us (98%)
  between operations  0.69 us (1%)
    pallas_call x1, Pallas kernels, on_device(): pl.pallas_call(gather_kernel, out_shape=(pltpu.VMEM((3, LAGS, CH, 128), B...  35.7 us
    pallas_call x1, Pallas kernels, swap(): pl.pallas_call(functools.partial(swap_kernel, code), out_shape=(pltpu.VME...  14 us
    pallas_call x1, Pallas kernels, on_device(): pl.pallas_call(write_kernel, out_shape=jax.ShapeDtypeStruct((LAGS, CH, 51...  4.72 us

profile of v1, /device:TPU:32, one launch (start us, length us, event | category | flops | bytes accessed | tf_op | source)
XLA Modules:
  0.0 55.2 jit_solution(9724672019981125314)
XLA Ops:
  0.7 14.0 %conditional.1 = ((bf16[2,16,2048]{2,1,0:T(8,128)(2,1)S(1)}, bf16[2,32,2048]{2,1,0:T(8,128)(2,1)S(1)})) conditional(s32[]{:T(128)} %clamp.3, bf16[16,16,256]{2,1,0:T(8,128)(2,1)} %param.11, bf16[16,16,256]{2,1,0:T(8,128)(2,1)} %param.11, bf16[16,16,256]{2,1,0:T(8,128)(2,1)} %param.11, ...), branch_computations={%region_0.1_spmd, %region_1.2_spmd, %region_2.3_spmd, %region_3.4_... | conditional | bytes 8 | solution.py:370
  0.7 14.0 %swap_1.1 = (bf16[2,16,2048]{2,1,0:T(8,128)(2,1)S(1)}, bf16[2,32,2048]{2,1,0:T(8,128)(2,1)S(1)}) custom-call(bf16[16,16,256]{2,1,0:T(8,128)(2,1)} %x_ref.1), custom_call_target="tpu_custom_call" | custom-call | tf_op jit(solution)/shard_map/cond/branch_1_fun/swap_1/pallas_call | solution.py:353
  14.7 35.7 %gather.1 = (bf16[3,768,16,128]{3,2,1,0:T(8,128)(2,1)S(1)}, bf16[2,8,256,256]{3,2,1,0:T(8,128)(2,1)S(1)}, bf16[2,400,256]{2,1,0:T(8,128)(2,1)S(1)}) custom-call(bf16[2,16,2048]{2,1,0:T(8,128)(2,1)S(1)} %get-tuple-element.18.own, bf16[2,32,2048]{2,1,0:T(8,128)(2,1)S(1)} %get-tuple-element.19.pair, bf16[2,400,256]{2,1,0:T(8,128)(2,1)} %constant.17.clone.table_hbm), custom_call_target="tpu_custom_call" | custom-call | tf_op jit(solution)/shard_map/gather/pallas_call | solution.py:371
  50.5 4.7 %write.1 = bf16[768,16,512]{2,1,0:T(8,128)(2,1)} custom-call(bf16[3,768,16,128]{3,2,1,0:T(8,128)(2,1)S(1)} %get-tuple-element.20.tiles, bf16[2,8,256,256]{3,2,1,0:T(8,128)(2,1)S(1)} %get-tuple-element.21.last, bf16[2,400,256]{2,1,0:T(8,128)(2,1)S(1)} %get-tuple-element.22.table), custom_call_target="tpu_custom_call" | custom-call | tf_op jit(solution)/shard_map/write/pallas_call | solution.py:392

commit v2 on v1

--- a/solution.py
+++ b/solution.py
@@ -68,7 +68,7 @@
         lax.fori_loop(0, 8, body, 0)
 
 
-def cross_half(whole, diag, cross, row, half):
+def cross_half(whole, diag, cross, row, half, beside=None):
     def body(g, carry):
         right = whole[half, pl.ds(row, 128), pl.ds(pl.multiple_of(g * 256, 256), 256)]
         gg = half * 8 + g
@@ -78,12 +78,14 @@
             for r in range(2):
                 r0 = c * 32 + r * 16
                 cross[r, c // 2, pl.ds(k0, 16), (c % 2) * 128 : (c % 2) * 128 + 128] = res[r0 : r0 + 16]
+        if beside is not None:
+            beside(g)
         return carry
 
     lax.fori_loop(0, 8, body, 0, unroll=8)
 
 
-def cross_pair(whole, diag, cross, row, row2, half):
+def cross_pair(whole, diag, cross, row, row2, half, beside=None):
     def body(g, carry):
         cols = pl.ds(pl.multiple_of(g * 256, 256), 256)
         right = jnp.concatenate([whole[half, pl.ds(row, 128), cols], whole[half, pl.ds(row2, 128), cols]], axis=0)
@@ -94,6 +96,8 @@
             for r in range(2):
                 r0 = c * 32 + r * 16
                 cross[r, c, pl.ds(k0, 16), :] = res[r0 : r0 + 16]
+        if beside is not None:
+            beside(g)
         return carry
 
     lax.fori_loop(0, 8, body, 0, unroll=8)
@@ -127,17 +131,24 @@
     lax.fori_loop(0, CH, body, 0, unroll=4)
 
 
-def finish(scr, out):
-    def body(i, carry):
-        d = pl.multiple_of(i * 16, 16)
-        out[pl.ds(HALF + d, 16)] = jnp.swapaxes(scr[0, :, pl.ds(d, 16), :], 0, 1)
-        earlier = jnp.swapaxes(scr[1, :, pl.ds(d, 16), :], 0, 1)
-        for u in range(16):
-            out[HALF - d - u] = earlier[u]
-        return carry
-
-    lax.fori_loop(0, HALF // 16, body, 0, unroll=2)
+def finish_step(scr, out, i):
+    d = pl.multiple_of(i * 16, 16)
+    out[pl.ds(HALF + d, 16)] = jnp.swapaxes(scr[0, :, pl.ds(d, 16), :], 0, 1)
+    earlier = jnp.swapaxes(scr[1, :, pl.ds(d, 16), :], 0, 1)
+    for u in range(16):
+        out[HALF - d - u] = earlier[u]
+
+
+def finish_end(scr, out):
     out[0] = jnp.swapaxes(scr[1, :, HALF : HALF + 16, :], 0, 1)[0]
+
+
+def finish_beside(scr, out):
+    def beside(g):
+        for u in range(3):
+            finish_step(scr, out, g * 3 + u)
+
+    return beside
 
 
 def flip(z_lo, bits):
@@ -205,7 +216,9 @@
             pair[half, pl.ds(same if side == 0 else far, 16), :] = land[side, half]
 
 
-def gather_kernel(own, pair, table_hbm, tiles, last, table, diag, whole, cross, scr, send_sem, recv_sem, table_sem):
+def gather_kernel(
+    own, pair, table_hbm, tile, scr, diag, far, table, whole, cross, scr0, send_sem, recv_sem, table_sem
+):
     grp, dev = lax.axis_index("grp"), lax.axis_index("dev")
     y, x, z_hi = dev // 8, lax.rem(dev // 2, 4), lax.rem(dev, 2)
 
@@ -267,20 +280,19 @@
 
     for half in range(2):
         send_full(half, 0, 0, 0)
+    build_diag(own, diag)
+    for half in range(2):
         send_full(half, 0, 0, 1)
-    build_diag(own, diag)
     for half in range(2):
         for a in (-1, 1):
             take(half, a, 0)
             forward(half, a, 0, 0)
             send_full(half, a, 0, 1)
-    for half in range(2):
-        for b in (-1, 1):
-            take(half, 0, b)
-            forward(half, 0, b, 1)
-    for half in range(2):
-        take(half, 2, 0)
-        send_full(half, 2, 0, 1)
+    for b in (-1, 1):
+        take(1, 0, b)
+        forward(1, 0, b, 1)
+    take(0, 2, 0)
+    send_full(0, 2, 0, 1)
 
     def row_of(dy):
         return pl.multiple_of(lax.rem(y + dy + 4, 4) * 128, 128)
@@ -288,36 +300,44 @@
     fetch.wait()
     first = cross.at[:, 0:8]
     cross_half(whole, diag, first, row_of(0), 0)
-    for half in range(2):
-        for a in (-1, 1):
-            for b in (-1, 1):
-                take(half, a, b)
-                forward(half, a, b, 1)
+    for a in (-1, 1):
+        for b in (-1, 1):
+            take(1, a, b)
+            forward(1, a, b, 1)
+    for b in (-1, 1):
+        take(0, 0, b)
+        forward(0, 0, b, 1)
+    take(1, 2, 0)
+    send_full(1, 2, 0, 1)
     arrive(1, 2, 0)
     cross_half(whole, diag, first, row_of(0), 1)
-    for half in range(2):
+    for a in (-1, 1):
         for b in (-1, 1):
-            take(half, 2, b)
-            forward(half, 2, b, 1)
-    lags_of(table, first, scr.at[0])
-    finish(scr.at[0], tiles.at[0])
-    cross_pair(whole, diag, cross, row_of(-1), row_of(1), 0)
+            take(0, a, b)
+            forward(0, a, b, 1)
+    lags_of(table, first, scr0)
+    for b in (-1, 1):
+        take(0, 2, b)
+        forward(0, 2, b, 1)
+    cross_pair(whole, diag, cross, row_of(-1), row_of(1), 0, finish_beside(scr0, tile))
+    finish_end(scr0, tile)
+    for b in (-1, 1):
+        take(1, 2, b)
+        forward(1, 2, b, 1)
     arrive(1, 2, -1)
     arrive(1, 2, 1)
     cross_pair(whole, diag, cross, row_of(-1), row_of(1), 1)
     lags_pair(table, cross, scr)
-    finish(scr.at[0], tiles.at[1])
-    finish(scr.at[1], tiles.at[2])
     for dx in OFFSETS:
         arrive(0, dx, 2)
-    cross_half(whole, diag, last, row_of(2), 0)
     arrive(1, 2, 2)
-    cross_half(whole, diag, last, row_of(2), 1)
+    for half in range(2):
+        far[half] = whole[half, pl.ds(row_of(2), 128), :]
     for c in started:
         c.wait_send()
 
 
-def write_kernel(tiles, last, table, out, scr, stage, sem):
+def write_kernel(tile, scr, diag, far, table, out, cross, scr0, stage, sem):
     y = lax.axis_index("dev") // 8
 
     def put(src, dy, k):
@@ -331,16 +351,43 @@
         ]
 
     copies = []
-    for i, dy in enumerate((0, -1, 1)):
-        copies += put(tiles.at[i], dy, i)
+
+    def write(src, dy):
+        mine = put(src, dy, len(copies) // PIECES)
+        for c in mine:
+            c.start()
+        copies.extend(mine)
+
+    write(tile, 0)
+    for half, dy in enumerate((-1, 1)):
+        cross_half(far, diag, cross, 0, half, finish_beside(scr.at[half], stage.at[half]))
+        finish_end(scr.at[half], stage.at[half])
+        write(stage.at[half], dy)
+    lags_of(table, cross, scr0)
+    lanes = pl.multiple_of(lax.rem(y + 2, 4) * 128, 128)
+    quarter = HALF // 4
+
+    def send_rows(first, count):
+        k = len(copies)
+        c = pltpu.make_async_copy(
+            stage.at[2, pl.ds(first, count)], out.at[pl.ds(first, count), :, pl.ds(lanes, 128)], sem.at[k]
+        )
+        c.start()
+        copies.append(c)
+
+    for q in range(4):
+
+        def body(i, carry, q=q):
+            finish_step(scr0, stage.at[2], q * (quarter // 16) + i)
+            return carry
+
+        lax.fori_loop(0, quarter // 16, body, 0, unroll=2)
+        if q == 3:
+            finish_end(scr0, stage.at[2])
+        send_rows(HALF + q * quarter, quarter)
+        low = HALF - (q + 1) * quarter + 1 if q < 3 else 0
+        send_rows(low, (HALF - q * quarter if q else HALF - 1) - low + 1)
     for c in copies:
-        c.start()
-    lags_of(table, last, scr)
-    finish(scr, stage)
-    final = put(stage, 2, 3)
-    for c in final:
-        c.start()
-    for c in copies + final:
         c.wait()
 
 
@@ -368,40 +415,42 @@
         )(block)
 
     own, pair = lax.switch(mask, [functools.partial(swap, code) for code in range(8)], spectra)
-    tiles, last, table = pl.pallas_call(
+    parts = pl.pallas_call(
         gather_kernel,
         out_shape=(
-            pltpu.VMEM((3, LAGS, CH, 128), BF16),
-            pltpu.VMEM((2, 8, NF, 256), BF16),
+            pltpu.VMEM((LAGS, CH, 128), BF16),
+            pltpu.VMEM((2, 2, CH, ROWS, 128), BF16),
+            pltpu.VMEM((16, 512, 256), BF16),
+            pltpu.VMEM((2, 128, 2048), BF16),
             pltpu.VMEM((2, ROWS, NF), BF16),
         ),
         in_specs=[vmem, vmem, pl.BlockSpec(memory_space=pltpu.HBM)],
-        out_specs=(vmem, vmem, vmem),
+        out_specs=(vmem,) * 5,
         scratch_shapes=[
-            pltpu.VMEM((16, 512, 256), BF16),
             pltpu.VMEM((2, 512, 2048), BF16),
             pltpu.VMEM((2, CH, NF, 256), BF16),
-            pltpu.VMEM((2, 2, CH, ROWS, 128), BF16),
+            pltpu.VMEM((2, CH, ROWS, 128), BF16),
             pltpu.SemaphoreType.DMA((len(KEYS),)),
             pltpu.SemaphoreType.DMA((len(KEYS),)),
             pltpu.SemaphoreType.DMA,
         ],
-        compiler_params=pltpu.CompilerParams(collective_id=8, has_side_effects=True, vmem_limit_bytes=24 * 2**20),
+        compiler_params=pltpu.CompilerParams(collective_id=8, has_side_effects=True, vmem_limit_bytes=16 * 2**20),
         name="gather",
     )(own, pair, pltpu.with_memory_space_constraint(table, pltpu.HBM))
     return pl.pallas_call(
         write_kernel,
         out_shape=jax.ShapeDtypeStruct((LAGS, CH, 512), BF16),
-        in_specs=[vmem] * 3,
+        in_specs=[vmem] * 5,
         out_specs=pl.BlockSpec(memory_space=pl.ANY),
         scratch_shapes=[
+            pltpu.VMEM((2, 8, NF, 256), BF16),
             pltpu.VMEM((2, CH, ROWS, 128), BF16),
-            pltpu.VMEM((LAGS, CH, 128), BF16),
-            pltpu.SemaphoreType.DMA((4 * PIECES,)),
+            pltpu.VMEM((3, LAGS, CH, 128), BF16),
+            pltpu.SemaphoreType.DMA((3 * PIECES + 8,)),
         ],
-        compiler_params=pltpu.CompilerParams(vmem_limit_bytes=24 * 2**20),
+        compiler_params=pltpu.CompilerParams(vmem_limit_bytes=20 * 2**20),
         name="write",
-    )(tiles, last, table)
+    )(*parts)
 
 
 def solution(mesh):

time: 55.3 us -> 53.6 us (0.969)
  the two profiles are of different devices: /device:TPU:32 before, /device:TPU:1 now
where the time goes in v2:
time: 53.6 us; the launch traced here: 53.5 us
  Pallas kernels  52.4 us (98%)
  between operations  0.85 us (2%)
    pallas_call x1, Pallas kernels, on_device(): pl.pallas_call(gather_kernel, out_shape=(pltpu.VMEM((LAGS, CH, 128), BF16...  29.5 us
    pallas_call x1, Pallas kernels, swap(): pl.pallas_call(functools.partial(swap_kernel, code), out_shape=(pltpu.VME...  16.6 us
    pallas_call x1, Pallas kernels, on_device(): pl.pallas_call(write_kernel, out_shape=jax.ShapeDtypeStruct((LAGS, CH, 51...  6.39 us

profile of v2, /device:TPU:1, one launch (start us, length us, event | category | flops | bytes accessed | tf_op | source)
XLA Modules:
  0.0 53.5 jit_solution(15858130312515135699)
XLA Ops:
  0.7 16.8 %conditional.1 = ((bf16[2,16,2048]{2,1,0:T(8,128)(2,1)S(1)}, bf16[2,32,2048]{2,1,0:T(8,128)(2,1)S(1)})) conditional(s32[]{:T(128)} %clamp.3, bf16[16,16,256]{2,1,0:T(8,128)(2,1)} %param.11, bf16[16,16,256]{2,1,0:T(8,128)(2,1)} %param.11, bf16[16,16,256]{2,1,0:T(8,128)(2,1)} %param.11, ...), branch_computations={%region_0.1_spmd, %region_1.2_spmd, %region_2.3_spmd, %region_3.4_... | conditional | bytes 8 | solution.py:417
  0.7 16.6 %swap_5.1 = (bf16[2,16,2048]{2,1,0:T(8,128)(2,1)S(1)}, bf16[2,32,2048]{2,1,0:T(8,128)(2,1)S(1)}) custom-call(bf16[16,16,256]{2,1,0:T(8,128)(2,1)} %x_ref.5), custom_call_target="tpu_custom_call" | custom-call | tf_op jit(solution)/shard_map/cond/branch_5_fun/swap_5/pallas_call | solution.py:400
  17.5 29.5 %gather.1 = (bf16[768,16,128]{2,1,0:T(8,128)(2,1)S(1)}, bf16[2,2,16,400,128]{4,3,2,1,0:T(8,128)(2,1)S(1)}, bf16[16,512,256]{2,1,0:T(8,128)(2,1)S(1)}, bf16[2,128...) custom-call(bf16[2,16,2048]{2,1,0:T(8,128)(2,1)S(1)} %get-tuple-element.20.own, ...), custom_call_target="tpu_custom_call" | custom-call | tf_op jit(solution)/shard_map/gather/pallas_call | solution.py:418
  47.0 6.4 %write.1 = bf16[768,16,512]{2,1,0:T(8,128)(2,1)} custom-call(bf16[768,16,128]{2,1,0:T(8,128)(2,1)S(1)} %get-tuple-element.22.tile, bf16[2,2,16,400,128]{4,3,2,1,0:T(8,128)(2,1)S(1)} %get-tuple-element.23.scr, bf16[16,512,256]{2,1,0:T(8,128)(2,1)S(1)} %get-tuple-element.24.diag, bf16[2,128,2048]{2,1,0:T(8,128)(2,1)S(1)} %get-tuple-element.25.far, ...), custom_call_target="tpu_custom_call" | custom-call | tf_op jit(solution)/shard_map/write/pallas_call | solution.py:440

commit v3 on v2

--- a/solution.py
+++ b/solution.py
@@ -233,6 +233,7 @@
         pl.semaphore_signal(barrier, inc=1, device_id=device, device_id_type=MESH)
     for half in range(2):
         whole[half, pl.ds(pl.multiple_of((y * 8 + x * 2) * 16, 32), 32), :] = pair[half]
+    build_diag(own, diag)
     pl.semaphore_wait(barrier, 4)
 
     started = []
@@ -280,7 +281,6 @@
 
     for half in range(2):
         send_full(half, 0, 0, 0)
-    build_diag(own, diag)
     for half in range(2):
         send_full(half, 0, 0, 1)
     for half in range(2):
@@ -300,15 +300,15 @@
     fetch.wait()
     first = cross.at[:, 0:8]
     cross_half(whole, diag, first, row_of(0), 0)
-    for a in (-1, 1):
-        for b in (-1, 1):
-            take(1, a, b)
-            forward(1, a, b, 1)
     for b in (-1, 1):
         take(0, 0, b)
         forward(0, 0, b, 1)
     take(1, 2, 0)
     send_full(1, 2, 0, 1)
+    for a in (-1, 1):
+        for b in (-1, 1):
+            take(1, a, b)
+            forward(1, a, b, 1)
     arrive(1, 2, 0)
     cross_half(whole, diag, first, row_of(0), 1)
     for a in (-1, 1):

time: 53.6 us -> 51.7 us (0.965)
  the two profiles are of different devices: /device:TPU:1 before, /device:TPU:32 now
where the time goes in v3:
time: 51.7 us; the launch traced here: 51.5 us
  Pallas kernels  50.5 us (98%)
  between operations  0.85 us (2%)
    pallas_call x1, Pallas kernels, on_device(): pl.pallas_call(gather_kernel, out_shape=(pltpu.VMEM((LAGS, CH, 128), BF16...  30.1 us
    pallas_call x1, Pallas kernels, swap(): pl.pallas_call(functools.partial(swap_kernel, code), out_shape=(pltpu.VME...  14 us
    pallas_call x1, Pallas kernels, on_device(): pl.pallas_call(write_kernel, out_shape=jax.ShapeDtypeStruct((LAGS, CH, 51...  6.4 us

profile of v3, /device:TPU:32, one launch (start us, length us, event | category | flops | bytes accessed | tf_op | source)
XLA Modules:
  0.0 51.5 jit_solution(8533653943551957943)
XLA Ops:
  0.7 14.2 %conditional.1 = ((bf16[2,16,2048]{2,1,0:T(8,128)(2,1)S(1)}, bf16[2,32,2048]{2,1,0:T(8,128)(2,1)S(1)})) conditional(s32[]{:T(128)} %clamp.3, bf16[16,16,256]{2,1,0:T(8,128)(2,1)} %param.11, bf16[16,16,256]{2,1,0:T(8,128)(2,1)} %param.11, bf16[16,16,256]{2,1,0:T(8,128)(2,1)} %param.11, ...), branch_computations={%region_0.1_spmd, %region_1.2_spmd, %region_2.3_spmd, %region_3.4_... | conditional | bytes 8 | solution.py:417
  0.7 14.0 %swap_6.1 = (bf16[2,16,2048]{2,1,0:T(8,128)(2,1)S(1)}, bf16[2,32,2048]{2,1,0:T(8,128)(2,1)S(1)}) custom-call(bf16[16,16,256]{2,1,0:T(8,128)(2,1)} %x_ref.6), custom_call_target="tpu_custom_call" | custom-call | tf_op jit(solution)/shard_map/cond/branch_6_fun/swap_6/pallas_call | solution.py:400
  14.9 30.1 %gather.1 = (bf16[768,16,128]{2,1,0:T(8,128)(2,1)S(1)}, bf16[2,2,16,400,128]{4,3,2,1,0:T(8,128)(2,1)S(1)}, bf16[16,512,256]{2,1,0:T(8,128)(2,1)S(1)}, bf16[2,128...) custom-call(bf16[2,16,2048]{2,1,0:T(8,128)(2,1)S(1)} %get-tuple-element.20.own, ...), custom_call_target="tpu_custom_call" | custom-call | tf_op jit(solution)/shard_map/gather/pallas_call | solution.py:418
  45.0 6.4 %write.1 = bf16[768,16,512]{2,1,0:T(8,128)(2,1)} custom-call(bf16[768,16,128]{2,1,0:T(8,128)(2,1)S(1)} %get-tuple-element.22.tile, bf16[2,2,16,400,128]{4,3,2,1,0:T(8,128)(2,1)S(1)} %get-tuple-element.23.scr, bf16[16,512,256]{2,1,0:T(8,128)(2,1)S(1)} %get-tuple-element.24.diag, bf16[2,128,2048]{2,1,0:T(8,128)(2,1)S(1)} %get-tuple-element.25.far, ...), custom_call_target="tpu_custom_call" | custom-call | tf_op jit(solution)/shard_map/write/pallas_call | solution.py:440
